TPU v7x, 32 devices: a whole 2x2x4 slice. The times are simulated.
32 devices in a mesh: seed: 4 (over x, core), chan: 2 (over y), fsdp: 4 (over z).
Axes of the slice: x: 2, y: 2, z: 4, core: 2. Of those that a mesh axis runs over, the one named last changes fastest.
Arguments:
- stream: bfloat16 [256, 144, 8192], P(('seed', 'fsdp'), None, 'chan'), parts along dimension 0, may hold values from -12.5 to 9.5
- mid: bfloat16 [256, 144, 2048], P(('seed', 'fsdp'), None, 'chan'), parts along dimension 0, may hold values from 0 to 2
- conv_weight: bfloat16 [8192, 8192], P(('seed', 'fsdp'), 'chan'), parts along dimension 0, may hold values from -0.125 to 0.125
- head_weight: bfloat16 [32768, 16384], P(('seed', 'chan'), 'fsdp'), parts along dimension 0, may hold values from -0.375 to 0.375
- labels: int32 [64], replicated, may hold values from 0 to 16383
- proj_act: bfloat16 [2048, 32], replicated, may hold values from -0.125 to 0.125
- proj_err: bfloat16 [8192, 64], P('chan'), may hold values from -6 to 6
Outputs:
- grad_proj: float32 [256, 2048], P(('seed', 'fsdp'), 'chan'), parts along dimension 0
There are 4 independent parts, one for each index of `seed`. A program takes and returns all parts, laid end to end along the dimension named above; an argument that names none is the same for every part. Nothing has to cross between parts.
All inputs are finite; a program needn't handle non-finite values.
Results may differ from a plain program's by a relative error of at most 0.01.
Values may be sent and summed in bfloat16 or wider, within the bound.
A program may use at most 192 MiB of HBM per device.

v0:
```python
import jax
import jax.numpy as jnp
from jax import lax
from jax.sharding import PartitionSpec as P


def per_device(stream, mid, conv_weight, head_weight, labels, proj_act, proj_err):
    images = stream.shape[0]
    positions = stream.shape[1]
    width = stream.shape[2]
    rows = images * positions
    gathered = lax.all_gather(mid, "chan", axis=2, tiled=True)
    mid_rows = gathered.reshape(rows, gathered.shape[2])
    conv_out = jnp.dot(
        mid_rows,
        lax.all_gather(conv_weight, "fsdp", axis=0, tiled=True),
        preferred_element_type=jnp.float32,
    )
    acts_proj = jnp.dot(mid_rows, proj_act, preferred_element_type=jnp.float32)
    y_local = stream.astype(jnp.float32) + conv_out.reshape(images, positions, width)
    pooled = jnp.mean(jnp.maximum(y_local, 0.0), axis=1).astype(jnp.bfloat16)
    pooled_all = lax.all_gather(pooled, "fsdp", axis=0, tiled=True)
    partial_value = jnp.dot(pooled_all, head_weight, preferred_element_type=jnp.float32)
    block = head_weight.shape[1]
    block_start = lax.axis_index("fsdp") * block
    logits = lax.psum(partial_value, "chan")
    expo = jnp.exp(logits)
    total = lax.psum(jnp.sum(expo, axis=1), "fsdp")
    classes = block_start + jnp.arange(block, dtype=jnp.int32)
    onehot = (labels[:, None] == classes[None, :]).astype(jnp.float32)
    dlogits = (expo / total[:, None] - onehot).astype(jnp.bfloat16)
    dpooled = lax.psum_scatter(
        lax.dot_general(
            dlogits, head_weight, (((1,), (1,)), ((), ())), preferred_element_type=jnp.float32
        ),
        "fsdp",
        scatter_dimension=0,
        tiled=True,
    )
    error = jnp.where(y_local > 0.0, dpooled[:, None, :] / positions, 0.0).astype(jnp.bfloat16)
    err_part = jnp.dot(error.reshape(rows, width), proj_err, preferred_element_type=jnp.float32)
    acts_cube = acts_proj.reshape(images, positions, acts_proj.shape[1])
    err_full = lax.psum(err_part.astype(jnp.bfloat16), "chan").astype(jnp.float32)
    grads = jnp.einsum(
        "npa,npb->nab",
        acts_cube,
        err_full.reshape(images, positions, err_full.shape[1]),
        precision=lax.Precision.HIGHEST,
    )
    grads = grads.reshape(images, -1)
    share = grads.shape[1] // lax.axis_size("chan")
    return lax.dynamic_slice_in_dim(grads, lax.axis_index("chan") * share, share, 1)


def solution(mesh):
    in_specs = (
        P(("seed", "fsdp"), None, "chan"),
        P(("seed", "fsdp"), None, "chan"),
        P(("seed", "fsdp"), "chan"),
        P(("seed", "chan"), "fsdp"),
        P(),
        P(),
        P("chan", None),
    )
    out_specs = P(("seed", "fsdp"), "chan")
    return jax.shard_map(
        per_device, mesh=mesh, in_specs=in_specs, out_specs=out_specs, check_vma=False
    )
```

profile of v0, /device:TPU:0, one launch (start us, length us, event | category | flops | bytes accessed | tf_op | source)
XLA Modules:
  0.0 668.9 jit_solution(1187256161833449838)
XLA Ops:
  6.5 0.0 copy-start
  6.5 0.0 all-gather.3.cloned.1.call-start
  6.5 0.7 all-gather.3.cloned.1.call-update
  7.3 0.0 all-gather.5.cloned.1.call-start
  7.3 0.7 all-gather.5.cloned.1.call-update
  8.0 0.0 all-reduce.3.cloned.1.call-start
  8.1 121.6 %all-gather.3.cloned.1.call-done = bf16[16,144,2048]{2,1,0:T(8,128)(2,1)} async-done(((bf16[16,144,1024]{2,1,0:T(8,128)(2,1)}), bf16[16,144,2048]{2,1,0:T(8,128)(2,1)}) %all-gather.3.cloned.1.call-update) | async-done | bytes 9437200 | tf_op jit(solution)/shard_map/all_gather | solution.py:12
  129.7 288.4 %all-gather.5.cloned.1.call-done = bf16[2048,4096]{1,0:T(8,128)(2,1)} async-done(((bf16[512,4096]{1,0:T(8,128)(2,1)}), bf16[2048,4096]{1,0:T(8,128)(2,1)}) %all-gather.5.cloned.1.call-update) | async-done | bytes 16777232 | tf_op jit(solution)/shard_map/all_gather | solution.py:16
  418.0 50.1 %maximum_reduce_fusion = (f32[16,4096]{1,0:T(8,128)S(1)}, f32[16,144,4096]{2,1,0:T(8,128)}) fusion(bf16[16,144,4096]{2,1,0:T(8,128)(2,1)} %param.7, bf16[16,144,2048]{2,1,0:T(8,128)(2,1)} %all-gather.3.cloned.1.call-done, bf16[2048,4096]{1,0:T(8,128)(2,1)} %all-gather.5.cloned.1.call-done), kind=kOutput, calls=%fused_computation.1 | convolution fusion | flops 38692388864 | bytes 83099648 | tf_op jit(solution)/shard_map/dot_general | solution.py:14
  468.1 16.2 %all_gather.11 = bf16[64,4096]{1,0:T(8,128)(2,1)S(1)} all-gather(bf16[16,4096]{1,0:T(8,128)(2,1)S(1)} %multiply_convert_fusion), channel_id=1, replica_groups=mesh['seed'=4,'chan'=2,'fsdp'=4] {'fsdp'}, dimensions={0}, use_global_device_ids=true | all-gather | bytes 655360 | tf_op jit(solution)/shard_map/all_gather | solution.py:22
  484.4 0.0 copy-start.2
  484.4 14.5 %fusion.8 = f32[64,4096]{1,0:T(8,128)} fusion(bf16[64,4096]{1,0:T(8,128)(2,1)S(1)} %all_gather.11, bf16[4096,4096]{1,0:T(8,128)(2,1)} %param.10), kind=kOutput, calls=%fused_computation.18 | convolution fusion | flops 2147483648 | bytes 35127296 | tf_op jit(solution)/shard_map/dot_general | solution.py:23
  498.9 0.0 all-reduce.3.cloned.1.call-update
  498.9 0.0 reduce-scatter.2.cloned.1.call-start
  499.0 38.5 %all-reduce.3.cloned.1.call-done = f32[64,4096]{1,0:T(8,128)} async-done(((f32[64,4096]{1,0:T(8,128)}), f32[64,4096]{1,0:T(8,128)}) %all-reduce.3.cloned.1.call-update) | async-done | bytes 1048592 | tf_op jit(solution)/shard_map/psum | solution.py:26
  537.5 1.5 exponential_reduce_fusion
  539.0 11.7 %psum.22 = f32[64]{0:T(128)S(1)} all-reduce(f32[64]{0:T(128)S(1)} %exponential_reduce_fusion), channel_id=1, replica_groups=mesh['seed'=4,'chan'=2,'fsdp'=4] {'fsdp'}, use_global_device_ids=true, to_apply=%region_3.0 | all-reduce | flops 64 | bytes 512 | tf_op jit(solution)/shard_map/psum | solution.py:28
  550.7 0.0 copy-done.2
  550.7 16.7 %fusion.2 = f32[64,4096]{1,0:T(8,128)} fusion(bf16[4096,4096]{1,0:T(8,128)(2,1)} %param.10, f32[64,4096]{1,0:T(8,128)} %all-reduce.3.cloned.1.call-done, s32[4096]{0:T(1024)S(1)} %iota_add_fusion, f32[64]{0:T(128)S(1)} %psum.22, s32[64]{0:T(128)S(1)} %copy-done.2), kind=kOutput, calls=%fused_computation.8 | convolution fusion | flops 2148794368 | bytes 35668480 | tf_op jit(solution)/shard_map/dot_general | solution.py:33
  567.4 0.0 reduce-scatter.2.cloned.1.call-update
  567.4 0.2 all-reduce.5.cloned.1.call-start
  567.6 24.3 %reduce-scatter.2.cloned.1.call-done = f32[16,4096]{1,0:T(8,128)} async-done(((f32[64,4096]{1,0:T(8,128)}), f32[16,4096]{1,0:T(8,128)}) %reduce-scatter.2.cloned.1.call-update) | async-done | bytes 262160 | tf_op jit(solution)/shard_map/reduce_scatter | solution.py:32
  591.9 1.0 broadcast_multiply_fusion
  592.9 25.7 %select_convert_fusion = bf16[16,144,4096]{2,1,0:T(8,128)(2,1)} fusion(f32[16,144,4096]{2,1,0:T(8,128)} %get-tuple-element.6, bf16[16,144,4096]{2,1,0:T(8,128)(2,1)} %param.7, bf16[16,4096]{1,0:T(8,128)(2,1)S(1)} %broadcast_multiply_fusion), kind=kLoop, calls=%fused_computation | loop fusion | flops 37748736 | bytes 75628544 | tf_op jit(solution)/shard_map/convert_element_type | solution.py:40
  618.5 0.0 copy-start.1
  618.5 0.0 copy-done
  618.5 12.2 %convolution_convert_fusion = bf16[2304,64]{0,1:T(8,128)(2,1)S(1)} fusion(bf16[2304,4096]{1,0:T(8,128)(2,1)} %bitcast.20, bf16[4096,64]{0,1:T(8,128)(2,1)S(1)} %copy-done), kind=kOutput, calls=%fused_computation.5 | convolution fusion | flops 1208107008 | bytes 19693568 | tf_op jit(solution)/shard_map/dot_general | solution.py:41
  630.8 0.9 reshape.25
  631.6 0.9 copy.8
  632.6 0.0 all-reduce.5.cloned.1.call-update
  632.6 0.0 copy-done.1
  632.6 6.9 %fusion.6 = f32[16,144,32]{1,2,0:T(8,128)S(1)} fusion(bf16[16,144,2048]{2,1,0:T(8,128)(2,1)} %all-gather.3.cloned.1.call-done, bf16[2048,32]{0,1:T(8,128)(2,1)S(1)} %copy-done.1), kind=kOutput, calls=%fused_computation.13 | convolution fusion | flops 301989888 | bytes 9863168 | tf_op jit(solution)/shard_map/dot_general | solution.py:19
  639.5 20.6 %all-reduce.5.cloned.1.call-done = bf16[16,144,64]{1,2,0:T(8,128)(2,1)} async-done(((bf16[16,144,64]{1,2,0:T(8,128)(2,1)}), bf16[16,144,64]{1,2,0:T(8,128)(2,1)}) %all-reduce.5.cloned.1.call-update) | async-done | bytes 294928 | tf_op jit(solution)/shard_map/psum | solution.py:43
  660.0 1.6 fusion.9
  661.6 0.1 reshape.26
  661.7 0.6 constant_dynamic-slice_fusion
  (2 shorter events, 0.0 us)
Async XLA Ops:
  6.5 612.0 %copy-start = (bf16[4096,64]{0,1:T(8,128)(2,1)S(1)}, bf16[4096,64]{0,1:T(8,128)(2,1)}, u32[]{:S(2)}) copy-start(bf16[4096,64]{0,1:T(8,128)(2,1)} %param.13) | copy-start | bytes 1572868
  6.5 123.1 %all-gather.3.cloned.1.call-start = ((), (), s32[]{:S(2)}) async-start(), calls=%async_computation.1 | async-start | bytes 14155776 | tf_op jit(solution)/shard_map/all_gather | solution.py:12
  7.3 410.8 %all-gather.5.cloned.1.call-start = ((), (), s32[]{:S(2)}) async-start(), calls=%async_computation.2 | async-start | bytes 20971520 | tf_op jit(solution)/shard_map/all_gather | solution.py:16
  8.0 529.5 %all-reduce.3.cloned.1.call-start = ((), (), s32[]{:S(2)}) async-start(), calls=%async_computation.3 | async-start | bytes 2097152 | tf_op jit(solution)/shard_map/psum | solution.py:26
  484.4 66.3 %copy-start.2 = (s32[64]{0:T(128)S(1)}, s32[64]{0:T(128)}, u32[]{:S(2)}) copy-start(s32[64]{0:T(128)} %param.11) | copy-start | bytes 772
  498.9 93.0 %reduce-scatter.2.cloned.1.call-start = ((), (), s32[]{:S(2)}) async-start(), calls=%async_computation.4 | async-start | bytes 1310720 | tf_op jit(solution)/shard_map/reduce_scatter | solution.py:32
  567.4 92.7 %all-reduce.5.cloned.1.call-start = ((), (), s32[]{:S(2)}) async-start(), calls=%async_computation.5 | async-start | bytes 1048576 | tf_op jit(solution)/shard_map/psum | solution.py:43
  618.5 14.1 %copy-start.1 = (bf16[2048,32]{0,1:T(8,128)(2,1)S(1)}, bf16[2048,32]{0,1:T(8,128)(2,1)}, u32[]{:S(2)}) copy-start(bf16[2048,32]{0,1:T(8,128)(2,1)} %param.12) | copy-start | bytes 393220
Sparse Core Ops, SparseCore 0:
  8.9 120.6 all-gather.2
  131.2 286.7 all-gather.4
  499.0 38.4 all-reduce.2
  567.5 24.3 reduce-scatter.1
  632.7 27.2 all-reduce.4
where the time goes:
time: 669 us
  waiting for transfers between devices  495 us (74%)
  matrix products  102 us (15%)
  other arithmetic  28.1 us (4%)
  blocking collectives  27.9 us (4%)
  between operations  13.2 us (2%)
    all_gather x1, waiting for transfers between devices, per_device(): lax.all_gather(conv_weight, 'fsdp', axis=0, tiled=True)  288 us
    all_gather x1, waiting for transfers between devices, per_device(): gathered = lax.all_gather(mid, 'chan', axis=2, tiled=True)  122 us
    dot_general x1, matrix products, per_device(): jnp.dot(mid_rows, lax.all_gather(conv_weight, 'fsdp', axis=0, tiled=True)...  50.1 us
    psum x1, waiting for transfers between devices, per_device(): logits = lax.psum(partial_value, 'chan')  38.5 us
    convert_element_type x1, other arithmetic, per_device(): jnp.where(y_local > 0.0, dpooled[:, None, :] / positions, 0.0)  25.7 us
    reduce_scatter x1, waiting for transfers between devices, per_device(): lax.psum_scatter(lax.dot_general(dlogits, head_weight, (((1,), (1,)), (()...  24.3 us
    psum x1, waiting for transfers between devices, per_device(): lax.psum(err_part.astype(jnp.bfloat16), 'chan').astype(jnp.float32)  20.6 us
    dot_general x1, matrix products, per_device(): lax.dot_general(dlogits, head_weight, (((1,), (1,)), ((), ())), preferred...  16.7 us
  transfers between devices with their start and end apart: 5, of which 5 were waited for; matrix products, arithmetic and copies ran while one was open for 1% of the time, Pallas kernels for 0%

commit v1 on v0

v1 whole, which is shorter than its diff:
```python
import functools

import jax
import jax.numpy as jnp
from jax import lax
from jax.experimental import pallas as pl
from jax.experimental.pallas import tpu as pltpu
from jax.sharding import PartitionSpec as P

MESH = pl.DeviceIdType.MESH
AHEAD = 3


def conv_kernel(
    nc, nf, positions, group,
    stream_ref, mid_ref, weight_ref, proj_ref,
    pooled_ref, cross_ref,
    weights, mids, acts, held,
    own_sem, right_sem, left_sem, in_sem, mid_send, mid_recv, mid_own, held_sem,
):
    c = lax.axis_index("chan")
    f = lax.axis_index("fsdp")
    chunks, depth, cw = weights.shape[1:]
    share = mids.shape[2]
    rows = mids.shape[1]
    images = rows // positions

    def own_copy(j):
        return pltpu.make_async_copy(
            weight_ref.at[:, pl.ds(pl.multiple_of(j * cw, cw), cw)], weights.at[f, j], own_sem.at[j]
        )

    def hop(b, j, right):
        return pltpu.make_async_remote_copy(
            src_ref=weights.at[b, j],
            dst_ref=weights.at[b, j],
            send_sem=(right_sem if right else left_sem).at[b, j],
            recv_sem=in_sem.at[b, j],
            device_id={"fsdp": f + 1 if right else f - 1},
            device_id_type=MESH,
        )

    def mid_copy(d):
        to = lax.rem(c + d, nc)
        return pltpu.make_async_remote_copy(
            src_ref=mid_ref,
            dst_ref=mids.at[c],
            send_sem=mid_send.at[d],
            recv_sem=mid_recv.at[d],
            device_id={"chan": to},
            device_id_type=MESH,
        )

    def stream_copy(k):
        slot = lax.rem(k, 2)
        return pltpu.make_async_copy(
            stream_ref.at[:, pl.ds(pl.multiple_of(k * cw, cw), cw)], held.at[slot], held_sem.at[slot]
        )

    lax.fori_loop(0, chunks, lambda j, x: (own_copy(j).start(), x)[1], 0)
    own_mid = pltpu.make_async_copy(mid_ref, mids.at[c], mid_own)
    own_mid.start()
    stream_copy(0).start()

    barrier = pltpu.get_barrier_semaphore()
    for d in range(1, nc):
        pl.semaphore_signal(barrier, 1, device_id={"chan": lax.rem(c + d, nc)}, device_id_type=MESH)

    @pl.when(f > 0)
    def _():
        pl.semaphore_signal(barrier, 1, device_id={"fsdp": f - 1}, device_id_type=MESH)

    @pl.when(f < nf - 1)
    def _():
        pl.semaphore_signal(barrier, 1, device_id={"fsdp": f + 1}, device_id_type=MESH)

    ends = jnp.where(f > 0, 1, 0) + jnp.where(f < nf - 1, 1, 0)
    pl.semaphore_wait(barrier, nc - 1 + ends)

    for d in range(1, nc):
        mid_copy(d).start()

    def send_own(j):
        own_copy(j).wait()

        @pl.when(f < nf - 1)
        def _():
            hop(f, j, True).start()

        @pl.when(f > 0)
        def _():
            hop(f, j, False).start()

    for j in range(min(AHEAD, chunks)):
        send_own(j)

    def relay(r):
        @pl.when(r + AHEAD < chunks)
        def _():
            send_own(r + AHEAD)

        for d in range(1, nf):
            @pl.when(f - d >= 0)
            def _():
                hop(f - d, r, True).wait_recv()

                @pl.when(f < nf - 1)
                def _():
                    hop(f - d, r, True).start()

            @pl.when(f + d < nf)
            def _():
                hop(f + d, r, False).wait_recv()

                @pl.when(f > 0)
                def _():
                    hop(f + d, r, False).start()

    step = min(depth, share)
    pieces = nf * depth // step

    def compute(k):
        stream_copy(k).wait()

        @pl.when(k + 1 < chunks)
        def _():
            stream_copy(k + 1).start()

        slot = lax.rem(k, 2)
        columns = pl.ds(pl.multiple_of(k * cw, cw), cw)

        def some(g, x):
            span = pl.ds(pl.multiple_of(g * group * positions, 16), group * positions)
            y = held[slot, span, :].astype(jnp.float32)
            for s in range(pieces):
                at = s * step
                y += jnp.dot(
                    mids[at // share, span, at % share : at % share + step],
                    weights[at // depth, k, at % depth : at % depth + step, :],
                    preferred_element_type=jnp.float32,
                )
            total = []
            for i in range(group):
                one = y[i * positions : (i + 1) * positions]
                total.append(jnp.sum(jnp.maximum(one, 0.0), axis=0, keepdims=True))
                mask = jnp.where(one > 0.0, 1.0, 0.0).astype(jnp.bfloat16)
                cross_ref[g * group + i, :, columns] = jnp.dot(
                    acts[g * group + i], mask, preferred_element_type=jnp.float32
                )
            mean = jnp.concatenate(total, axis=0) / positions
            pooled_ref[g, :, columns] = mean
            return x

        lax.fori_loop(0, images // group, some, 0)

    def project():
        own_mid.wait()
        for d in range(1, nc):
            mid_copy(d).wait_recv()

        def one(i, x):
            span = pl.ds(pl.multiple_of(i * positions, 16), positions)
            out = jnp.zeros((proj_ref.shape[0], positions), jnp.float32)
            for q in range(nc):
                out += lax.dot_general(
                    proj_ref[:, q * share : (q + 1) * share], mids[q, span, :],
                    (((1,), (1,)), ((), ())), preferred_element_type=jnp.float32,
                )
            acts[i] = out.astype(jnp.bfloat16)
            return x

        lax.fori_loop(0, images, one, 0)

    first = max(chunks // 2 - 1, 0)
    last = max(chunks - 2, 0)
    lax.fori_loop(0, first, lambda r, x: (relay(r), x)[1], 0)
    project()

    def pair(r, x):
        relay(r)
        compute(2 * (r - first))
        compute(2 * (r - first) + 1)
        return x

    lax.fori_loop(first, last, pair, 0)

    def single(r, x):
        relay(r)
        compute(r)
        return x

    lax.fori_loop(last, chunks, single, 0)

    def drain(j, x):
        @pl.when(f < nf - 1)
        def _():
            hop(f, j, True).wait_send()

        @pl.when(f > 0)
        def _():
            hop(f, j, False).wait_send()

        for d in range(1, nf):
            @pl.when((f - d >= 0) & (f < nf - 1))
            def _():
                hop(f - d, j, True).wait_send()

            @pl.when((f + d < nf) & (f > 0))
            def _():
                hop(f + d, j, False).wait_send()

        return x

    lax.fori_loop(0, chunks, drain, 0)
    for d in range(1, nc):
        mid_copy(d).wait_send()


def conv(stream, mid, weight, proj_t, nc, nf):
    images, positions, width = stream.shape
    rows = images * positions
    share = mid.shape[2]
    depth = weight.shape[0]
    ka = proj_t.shape[0]
    cw = min(256, width)
    chunks = width // cw
    group = 4
    vmem = pl.BlockSpec(memory_space=pltpu.VMEM)
    hbm = pl.BlockSpec(memory_space=pl.ANY)
    dma = pltpu.SemaphoreType.DMA
    pooled, cross = pl.pallas_call(
        functools.partial(conv_kernel, nc, nf, positions, group),
        out_shape=(
            jax.ShapeDtypeStruct((images // group, group, width), jnp.float32),
            jax.ShapeDtypeStruct((images, ka, width), jnp.float32),
        ),
        in_specs=[hbm, hbm, hbm, vmem],
        out_specs=(vmem, vmem),
        scratch_shapes=[
            pltpu.VMEM((nf, chunks, depth, cw), jnp.bfloat16),
            pltpu.VMEM((nc, rows, share), jnp.bfloat16),
            pltpu.VMEM((images, ka, positions), jnp.bfloat16),
            pltpu.VMEM((2, rows, cw), jnp.bfloat16),
            dma((chunks,)),
            dma((nf, chunks)),
            dma((nf, chunks)),
            dma((nf, chunks)),
            dma((nc,)),
            dma((nc,)),
            dma,
            dma((2,)),
        ],
        compiler_params=pltpu.CompilerParams(
            collective_id=0, has_side_effects=True, vmem_limit_bytes=56 * 2**20
        ),
        cost_estimate=pl.CostEstimate(
            flops=2 * rows * width * depth * nf,
            bytes_accessed=2 * rows * width + 2 * depth * nf * width,
            transcendentals=0,
        ),
    )(stream.reshape(rows, width), mid.reshape(rows, share), weight, proj_t)
    return pooled.reshape(images, width).astype(jnp.bfloat16), cross


def per_device(nc, nf, stream, mid, conv_weight, head_weight, labels, proj_act, proj_err):
    images, positions, width = stream.shape
    pooled, cross = conv(stream, mid, conv_weight, proj_act.T, nc, nf)
    pooled_all = lax.all_gather(pooled, "fsdp", axis=0, tiled=True)
    partial_value = jnp.dot(pooled_all, head_weight, preferred_element_type=jnp.float32)
    block = head_weight.shape[1]
    block_start = lax.axis_index("fsdp") * block
    logits = lax.psum(partial_value, "chan")
    expo = jnp.exp(logits)
    total = lax.psum(jnp.sum(expo, axis=1), "fsdp")
    classes = block_start + jnp.arange(block, dtype=jnp.int32)
    onehot = (labels[:, None] == classes[None, :]).astype(jnp.float32)
    dlogits = (expo / total[:, None] - onehot).astype(jnp.bfloat16)
    dpooled = lax.psum_scatter(
        lax.dot_general(
            dlogits, head_weight, (((1,), (1,)), ((), ())), preferred_element_type=jnp.float32
        ),
        "fsdp",
        scatter_dimension=0,
        tiled=True,
    )
    error = (dpooled / positions).astype(jnp.bfloat16).astype(jnp.float32)
    scaled = (cross * error[:, None, :]).astype(jnp.bfloat16)
    ka = cross.shape[1]
    grads = jnp.dot(
        scaled.reshape(images * ka, width), proj_err, preferred_element_type=jnp.float32
    ).reshape(images, ka * proj_err.shape[1])
    return lax.psum_scatter(grads, "chan", scatter_dimension=1, tiled=True)


def solution(mesh):
    in_specs = (
        P(("seed", "fsdp"), None, "chan"),
        P(("seed", "fsdp"), None, "chan"),
        P(("seed", "fsdp"), "chan"),
        P(("seed", "chan"), "fsdp"),
        P(),
        P(),
        P("chan", None),
    )
    out_specs = P(("seed", "fsdp"), "chan")
    return jax.shard_map(
        functools.partial(per_device, mesh.shape["chan"], mesh.shape["fsdp"]),
        mesh=mesh, in_specs=in_specs, out_specs=out_specs, check_vma=False,
    )
```

time: 669 us -> 441 us (0.66)
  waiting for transfers between devices: 495 us -> 72.8 us
  Pallas kernels: 0 us -> 286 us
  matrix products: 102 us -> 32.5 us
  other arithmetic: 28.1 us -> 7.92 us
    all_gather x2 -> x0, waiting for transfers between devices: 410 us -> none  [the longest x1 288 us: per_device(): lax.all_gather(conv_weight, 'fsdp', axis=0, tiled=True)]
    pallas_call x0 -> x1, Pallas kernels: none -> 286 us  [conv(): pl.pallas_call(functools.partial(conv_kernel, nc, nf, positions, group),...]
    dot_general x4 -> x1, matrix products: 70.7 us -> 1.23 us  [per_device(): jnp.dot(scaled.reshape(images * ka, width), proj_err, preferred_element_t...]
    psum x1 -> x0, waiting for transfers between devices: 20.6 us -> none  [per_device(): lax.psum(err_part.astype(jnp.bfloat16), 'chan').astype(jnp.float32)]
    convert_element_type x2 -> x3, other arithmetic: 25.7 us -> 6.43 us  [the longest x1 4.46 us: per_device(): scaled = (cross * error[:, None, :]).astype(jnp.bfloat16)]
    reduce_scatter x0 -> x1, waiting for transfers between devices: none -> 9.06 us  [per_device(): return lax.psum_scatter(grads, 'chan', scatter_dimension=1, tiled=True)]
  transfers between devices with their start and end apart: 5 -> 3, of which waited for: 5 -> 3; matrix products, arithmetic and copies ran while one was open for 1% -> 0% of each run, Pallas kernels for 0% -> 0%
where the time goes in v1:
time: 441 us
  Pallas kernels  286 us (65%)
  waiting for transfers between devices  72.8 us (17%)
  matrix products  32.5 us (7%)
  blocking collectives  27.5 us (6%)
  between operations  13.2 us (3%)
  other arithmetic  7.92 us (2%)
    pallas_call x1, Pallas kernels, conv(): pl.pallas_call(functools.partial(conv_kernel, nc, nf, positions, group),...  286 us
    psum x1, waiting for transfers between devices, per_device(): logits = lax.psum(partial_value, 'chan')  39.2 us
    reduce_scatter x1, waiting for transfers between devices, per_device(): lax.psum_scatter(lax.dot_general(dlogits, head_weight, (((1,), (1,)), (()...  24.5 us
    dot_general x1, matrix products, per_device(): lax.dot_general(dlogits, head_weight, (((1,), (1,)), ((), ())), preferred...  16.7 us
    all_gather x1, blocking collectives, per_device(): pooled_all = lax.all_gather(pooled, 'fsdp', axis=0, tiled=True)  15.8 us
    dot_general x1, matrix products, per_device(): jnp.dot(pooled_all, head_weight, preferred_element_type=jnp.float32)  14.6 us
    psum x1, blocking collectives, per_device(): total = lax.psum(jnp.sum(expo, axis=1), 'fsdp')  11.7 us
    reduce_scatter x1, waiting for transfers between devices, per_device(): return lax.psum_scatter(grads, 'chan', scatter_dimension=1, tiled=True)  9.06 us
  transfers between devices with their start and end apart: 3, of which 3 were waited for; matrix products, arithmetic and copies ran while one was open for 0% of the time, Pallas kernels for 0%

profile of v1, /device:TPU:0, one launch (start us, length us, event | category | flops | bytes accessed | tf_op | source)
XLA Modules:
  0.0 441.2 jit_solution(17373475656224381407)
XLA Ops:
  6.5 0.0 copy-start
  6.5 0.0 all-reduce.2.cloned.1.call-start
  6.5 286.4 %shard_map.73 = (f32[4,4,4096]{2,1,0:T(4,128)}, f32[16,32,4096]{2,1,0:T(8,128)}) custom-call(bf16[2304,4096]{1,0:T(8,128)(2,1)} %bitcast.10, bf16[2304,1024]{1,0:T(8,128)(2,1)} %bitcast.11, bf16[512,4096]{1,0:T(8,128)(2,1)} %weight_ref.1, bf16[32,2048]{1,0:T(8,128)(2,1)} %bitcast.12), custom_call_target="tpu_custom_call" | custom-call | flops 38654705664 | bytes 35651584 | tf_op jit(solution)/shard_map/pallas_call | solution.py:231
  293.0 1.0 convert_element_type.21
  294.0 15.8 %all_gather.3 = bf16[64,4096]{1,0:T(8,128)(2,1)S(1)} all-gather(bf16[16,4096]{1,0:T(8,128)(2,1)S(1)} %convert_element_type.22), channel_id=1, replica_groups=mesh['seed'=4,'chan'=2,'fsdp'=4] {'fsdp'}, dimensions={0}, use_global_device_ids=true | all-gather | bytes 655360 | tf_op jit(solution)/shard_map/all_gather | solution.py:268
  309.8 0.0 copy-start.1
  309.8 14.6 %fusion.5 = f32[64,4096]{1,0:T(8,128)} fusion(bf16[64,4096]{1,0:T(8,128)(2,1)S(1)} %all_gather.3, bf16[4096,4096]{1,0:T(8,128)(2,1)} %param.10), kind=kOutput, calls=%fused_computation.10 | convolution fusion | flops 2147483648 | bytes 35127296 | tf_op jit(solution)/shard_map/dot_general | solution.py:269
  324.4 0.0 all-reduce.2.cloned.1.call-update
  324.4 0.0 reduce-scatter.3.cloned.1.call-start
  324.5 39.2 %all-reduce.2.cloned.1.call-done = f32[64,4096]{1,0:T(8,128)} async-done(((f32[64,4096]{1,0:T(8,128)}), f32[64,4096]{1,0:T(8,128)}) %all-reduce.2.cloned.1.call-update) | async-done | bytes 1048592 | tf_op jit(solution)/shard_map/psum | solution.py:272
  363.7 1.5 exponential_reduce_fusion
  365.1 11.7 %psum.15 = f32[64]{0:T(128)S(1)} all-reduce(f32[64]{0:T(128)S(1)} %exponential_reduce_fusion), channel_id=1, replica_groups=mesh['seed'=4,'chan'=2,'fsdp'=4] {'fsdp'}, use_global_device_ids=true, to_apply=%region_2.0 | all-reduce | flops 64 | bytes 512 | tf_op jit(solution)/shard_map/psum | solution.py:274
  376.8 0.0 copy-done.1
  376.8 16.7 %fusion = f32[64,4096]{1,0:T(8,128)} fusion(bf16[4096,4096]{1,0:T(8,128)(2,1)} %param.10, f32[64,4096]{1,0:T(8,128)} %all-reduce.2.cloned.1.call-done, s32[4096]{0:T(1024)S(1)} %iota_add_fusion, f32[64]{0:T(128)S(1)} %psum.15, s32[64]{0:T(128)S(1)} %copy-done.1), kind=kOutput, calls=%fused_computation.3 | convolution fusion | flops 2148794368 | bytes 35668480 | tf_op jit(solution)/shard_map/dot_general | solution.py:279
  393.5 0.0 reduce-scatter.3.cloned.1.call-update
  393.5 0.0 reduce-scatter.5.cloned.1.call-start
  393.6 24.5 %reduce-scatter.3.cloned.1.call-done = f32[16,4096]{1,0:T(8,128)} async-done(((f32[64,4096]{1,0:T(8,128)}), f32[16,4096]{1,0:T(8,128)}) %reduce-scatter.3.cloned.1.call-update) | async-done | bytes 262160 | tf_op jit(solution)/shard_map/reduce_scatter | solution.py:278
  418.1 1.0 fusion.4
  419.1 4.5 %multiply_convert_fusion = bf16[16,32,4096]{2,1,0:T(8,128)(2,1)S(1)} fusion(f32[16,32,4096]{2,1,0:T(8,128)} %get-tuple-element.7, f32[16,4096]{1,0:T(8,128)S(1)} %fusion.4), kind=kLoop, calls=%fused_computation | loop fusion | flops 4194304 | bytes 12845056 | tf_op jit(solution)/shard_map/convert_element_type | solution.py:287
  423.5 0.0 copy-done
  423.6 1.2 fusion.6
  424.8 0.8 reshape.24
  425.5 0.0 reduce-scatter.5.cloned.1.call-update
  425.6 9.1 %reduce-scatter.5.cloned.1.call-done = f32[16,1024]{1,0:T(8,128)} async-done(((f32[16,2048]{1,0:T(8,128)}), f32[16,1024]{1,0:T(8,128)}) %reduce-scatter.5.cloned.1.call-update) | async-done | bytes 65552 | tf_op jit(solution)/shard_map/reduce_scatter | solution.py:292
  (2 shorter events, 0.0 us)
Async XLA Ops:
  6.5 417.0 %copy-start = (bf16[4096,64]{0,1:T(8,128)(2,1)S(1)}, bf16[4096,64]{0,1:T(8,128)(2,1)}, u32[]{:S(2)}) copy-start(bf16[4096,64]{0,1:T(8,128)(2,1)} %param.13) | copy-start | bytes 1572868
  6.5 357.1 %all-reduce.2.cloned.1.call-start = ((), (), s32[]{:S(2)}) async-start(), calls=%async_computation.2 | async-start | bytes 2097152 | tf_op jit(solution)/shard_map/psum | solution.py:272
  309.8 67.0 %copy-start.1 = (s32[64]{0:T(128)S(1)}, s32[64]{0:T(128)}, u32[]{:S(2)}) copy-start(s32[64]{0:T(128)} %param.11) | copy-start | bytes 772
  324.4 93.7 %reduce-scatter.3.cloned.1.call-start = ((), (), s32[]{:S(2)}) async-start(), calls=%async_computation.3 | async-start | bytes 1310720 | tf_op jit(solution)/shard_map/reduce_scatter | solution.py:278
  393.5 41.1 %reduce-scatter.5.cloned.1.call-start = ((), (), s32[]{:S(2)}) async-start(), calls=%async_computation.4 | async-start | bytes 196608 | tf_op jit(solution)/shard_map/reduce_scatter | solution.py:292
Sparse Core Ops, SparseCore 0:
  324.5 39.0 all-reduce.1
  393.7 24.3 reduce-scatter.2
  425.7 8.8 reduce-scatter.4

commit v2 on v1

--- a/solution.py
+++ b/solution.py
@@ -11,12 +11,15 @@
 AHEAD = 3
 
 
-def conv_kernel(
+def trak_kernel(
     nc, nf, positions, group,
-    stream_ref, mid_ref, weight_ref, proj_ref,
-    pooled_ref, cross_ref,
-    weights, mids, acts, held,
+    stream_ref, mid_ref, weight_ref, proj_ref, head_ref, labels_ref, perr_ref,
+    out_ref,
+    weights, mids, acts, held, cross, mean, pools, heads, logits, logits_in,
+    totals, dlogits, dpool, dpool_in, perr, grads, shares, shares_in,
     own_sem, right_sem, left_sem, in_sem, mid_send, mid_recv, mid_own, held_sem,
+    pool_send, pool_recv, head_sem, logit_send, logit_recv, total_send, total_recv,
+    dlog_send, dlog_recv, dpool_send, dpool_recv, perr_sem, share_send, share_recv,
 ):
     c = lax.axis_index("chan")
     f = lax.axis_index("fsdp")
@@ -62,20 +65,66 @@
     own_mid.start()
     stream_copy(0).start()
 
+    classes = head_ref.shape[1]
+    tile = min(1024, classes)
+    slots = heads.shape[0]
+    part = logits.shape[1]
+
+    def head_copy(t):
+        slot = lax.rem(t, slots)
+        return pltpu.make_async_copy(
+            head_ref.at[pl.ds(pl.multiple_of(lax.rem(t, chunks) * cw, cw), cw), :],
+            heads.at[slot], head_sem.at[slot],
+        )
+
+    def to_chan(src, dst, send, recv, d):
+        return pltpu.make_async_remote_copy(
+            src_ref=src, dst_ref=dst, send_sem=send.at[d], recv_sem=recv.at[d],
+            device_id={"chan": lax.rem(c + d, nc)}, device_id_type=MESH,
+        )
+
+    def to_fsdp(src, dst, send, recv, d):
+        return pltpu.make_async_remote_copy(
+            src_ref=src, dst_ref=dst, send_sem=send, recv_sem=recv,
+            device_id={"fsdp": lax.rem(f + d, nf)}, device_id_type=MESH,
+        )
+
+    def pool_copy(k, d):
+        return to_fsdp(pools.at[k, f], pools.at[k, f], pool_send.at[d, k], pool_recv.at[d, k], d)
+
+    def logit_copy(d):
+        return to_chan(logits.at[lax.rem(c + d, nc)], logits_in.at[c], logit_send, logit_recv, d)
+
+    def total_copy(d):
+        return to_fsdp(totals.at[f], totals.at[f], total_send.at[d], total_recv.at[d], d)
+
+    def dlog_copy(d):
+        return to_chan(dlogits.at[c], dlogits.at[c], dlog_send, dlog_recv, d)
+
+    def dpool_copy(k, d):
+        return to_fsdp(
+            dpool.at[k, lax.rem(f + d, nf)], dpool_in.at[k, f], dpool_send.at[d, k], dpool_recv.at[d, k], d
+        )
+
+    def share_copy(d):
+        return to_chan(shares.at[lax.rem(c + d, nc)], shares_in.at[c], share_send, share_recv, d)
+
+    for t in range(slots):
+        head_copy(t).start()
+    perr_copy = pltpu.make_async_copy(perr_ref, perr.at[0 : perr_ref.shape[0]], perr_sem)
+    perr_copy.start()
+    perr[perr_ref.shape[0] :] = jnp.zeros(
+        (perr.shape[0] - perr_ref.shape[0], perr.shape[1]), perr.dtype
+    )
+    logits[...] = jnp.zeros_like(logits)
+
     barrier = pltpu.get_barrier_semaphore()
     for d in range(1, nc):
         pl.semaphore_signal(barrier, 1, device_id={"chan": lax.rem(c + d, nc)}, device_id_type=MESH)
 
-    @pl.when(f > 0)
-    def _():
-        pl.semaphore_signal(barrier, 1, device_id={"fsdp": f - 1}, device_id_type=MESH)
-
-    @pl.when(f < nf - 1)
-    def _():
-        pl.semaphore_signal(barrier, 1, device_id={"fsdp": f + 1}, device_id_type=MESH)
-
-    ends = jnp.where(f > 0, 1, 0) + jnp.where(f < nf - 1, 1, 0)
-    pl.semaphore_wait(barrier, nc - 1 + ends)
+    for d in range(1, nf):
+        pl.semaphore_signal(barrier, 1, device_id={"fsdp": lax.rem(f + d, nf)}, device_id_type=MESH)
+    pl.semaphore_wait(barrier, nc - 1 + nf - 1)
 
     for d in range(1, nc):
         mid_copy(d).start()
@@ -127,7 +176,6 @@
             stream_copy(k + 1).start()
 
         slot = lax.rem(k, 2)
-        columns = pl.ds(pl.multiple_of(k * cw, cw), cw)
 
         def some(g, x):
             span = pl.ds(pl.multiple_of(g * group * positions, 16), group * positions)
@@ -139,19 +187,37 @@
                     weights[at // depth, k, at % depth : at % depth + step, :],
                     preferred_element_type=jnp.float32,
                 )
-            total = []
             for i in range(group):
                 one = y[i * positions : (i + 1) * positions]
-                total.append(jnp.sum(jnp.maximum(one, 0.0), axis=0, keepdims=True))
+                total = jnp.sum(jnp.maximum(one, 0.0), axis=0, keepdims=True)
+                mean[pl.ds(g * group + i, 1), :] = total / positions
                 mask = jnp.where(one > 0.0, 1.0, 0.0).astype(jnp.bfloat16)
-                cross_ref[g * group + i, :, columns] = jnp.dot(
+                cross[k, g * group + i] = jnp.dot(
                     acts[g * group + i], mask, preferred_element_type=jnp.float32
-                )
-            mean = jnp.concatenate(total, axis=0) / positions
-            pooled_ref[g, :, columns] = mean
+                ).astype(cross.dtype)
             return x
 
         lax.fori_loop(0, images // group, some, 0)
+        pools[k, f] = mean[...].astype(jnp.bfloat16)
+        for d in range(1, nf):
+            pool_copy(k, d).start()
+
+    def add_logits(k):
+        head_copy(k).wait()
+        for d in range(1, nf):
+            pool_copy(k, d).wait_recv()
+        slot = lax.rem(k, slots)
+        rows_all = pools[k].reshape(nf * images, cw)
+
+        def some(g, x):
+            span = pl.ds(pl.multiple_of(g * tile, tile), tile)
+            add = jnp.dot(rows_all, heads[slot, :, span], preferred_element_type=jnp.float32)
+            for q in range(nc):
+                logits[q, :, span] += add[q * part : (q + 1) * part]
+            return x
+
+        lax.fori_loop(0, classes // tile, some, 0)
+        head_copy(k + slots).start()
 
     def project():
         own_mid.wait()
@@ -180,6 +246,12 @@
         relay(r)
         compute(2 * (r - first))
         compute(2 * (r - first) + 1)
+
+        @pl.when(r > first)
+        def _():
+            add_logits(2 * (r - first) - 2)
+            add_logits(2 * (r - first) - 1)
+
         return x
 
     lax.fori_loop(first, last, pair, 0)
@@ -187,9 +259,107 @@
     def single(r, x):
         relay(r)
         compute(r)
+
+        @pl.when(r >= 2)
+        def _():
+            add_logits(r - 2)
+
         return x
 
     lax.fori_loop(last, chunks, single, 0)
+    for k in range(last, chunks):
+        add_logits(k)
+
+    for d in range(1, nc):
+        logit_copy(d).start()
+    for d in range(1, nc):
+        logit_copy(d).wait_recv()
+
+    def exponents(g, total):
+        span = pl.ds(pl.multiple_of(g * tile, tile), tile)
+        value = logits[c, :, span]
+        for d in range(1, nc):
+            value += logits_in[lax.rem(c + nc - d, nc), :, span]
+        value = jnp.exp(value)
+        logits[c, :, span] = value
+        return total + jnp.sum(value, axis=1, keepdims=True)
+
+    total = lax.fori_loop(0, classes // tile, exponents, jnp.zeros((part, 1), jnp.float32))
+    totals[f] = jnp.broadcast_to(total, totals.shape[1:])
+    for d in range(1, nf):
+        total_copy(d).start()
+    for d in range(1, nf):
+        total_copy(d).wait_recv()
+    total = jnp.sum(totals[...], axis=0)[:, :1]
+
+    def derivatives(g, x):
+        span = pl.ds(pl.multiple_of(g * tile, tile), tile)
+        ids = f * classes + g * tile + lax.broadcasted_iota(jnp.int32, (part, tile), 1)
+        onehot = jnp.where(labels_ref[c] == ids, 1.0, 0.0)
+        dlogits[c, :, span] = (logits[c, :, span] / total - onehot).astype(dlogits.dtype)
+        return x
+
+    lax.fori_loop(0, classes // tile, derivatives, 0)
+    for d in range(1, nc):
+        dlog_copy(d).start()
+    for d in range(1, nc):
+        dlog_copy(d).wait_recv()
+
+    def back(k, x):
+        head_copy(k + chunks).wait()
+        slot = lax.rem(k + chunks, slots)
+        grad = lax.dot_general(
+            dlogits[...].reshape(nc * part, classes).astype(jnp.bfloat16), heads[slot],
+            (((1,), (1,)), ((), ())), preferred_element_type=jnp.float32,
+        )
+        dpool[k] = grad.reshape(nf, images, cw).astype(jnp.bfloat16)
+        for d in range(1, nf):
+            dpool_copy(k, d).start()
+
+        @pl.when(k + slots < chunks)
+        def _():
+            head_copy(k + chunks + slots).start()
+
+        return x
+
+    lax.fori_loop(0, chunks, back, 0)
+    perr_copy.wait()
+    grads[...] = jnp.zeros_like(grads)
+
+    def finish(k, x):
+        error = dpool[k, f].astype(jnp.float32)
+        for d in range(1, nf):
+            dpool_copy(k, d).wait_recv()
+        for d in range(1, nf):
+            error += dpool_in[k, lax.rem(f + nf - d, nf)].astype(jnp.float32)
+        error = (error / positions).astype(jnp.bfloat16).astype(jnp.float32)
+        scaled = jnp.concatenate(
+            [
+                (cross[k, i].astype(jnp.float32) * error[i : i + 1]).astype(jnp.bfloat16)
+                for i in range(images)
+            ],
+            axis=0,
+        )
+        grads[...] += lax.dot_general(
+            scaled, perr[:, pl.ds(pl.multiple_of(k * cw, cw), cw)],
+            (((1,), (1,)), ((), ())), preferred_element_type=jnp.float32,
+        )
+        return x
+
+    lax.fori_loop(0, chunks, finish, 0)
+    ka = proj_ref.shape[0]
+    kq = ka // nc
+    for q in range(nc):
+        for i in range(images):
+            shares[q, i] = grads[i * ka + q * kq : i * ka + (q + 1) * kq]
+    for d in range(1, nc):
+        share_copy(d).start()
+    for d in range(1, nc):
+        share_copy(d).wait_recv()
+    result = shares[c]
+    for d in range(1, nc):
+        result += shares_in[lax.rem(c + nc - d, nc)]
+    out_ref[...] = result
 
     def drain(j, x):
         @pl.when(f < nf - 1)
@@ -201,6 +371,9 @@
             hop(f, j, False).wait_send()
 
         for d in range(1, nf):
+            pool_copy(j, d).wait_send()
+            dpool_copy(j, d).wait_send()
+
             @pl.when((f - d >= 0) & (f < nf - 1))
             def _():
                 hop(f - d, j, True).wait_send()
@@ -214,33 +387,56 @@
     lax.fori_loop(0, chunks, drain, 0)
     for d in range(1, nc):
         mid_copy(d).wait_send()
-
-
-def conv(stream, mid, weight, proj_t, nc, nf):
+        logit_copy(d).wait_send()
+        dlog_copy(d).wait_send()
+        share_copy(d).wait_send()
+    for d in range(1, nf):
+        total_copy(d).wait_send()
+
+
+def per_device(nc, nf, stream, mid, conv_weight, head_weight, labels, proj_act, proj_err):
     images, positions, width = stream.shape
     rows = images * positions
     share = mid.shape[2]
-    depth = weight.shape[0]
-    ka = proj_t.shape[0]
+    depth = conv_weight.shape[0]
+    ka, ke = proj_act.shape[1], proj_err.shape[1]
+    classes = head_weight.shape[1]
+    everyone = images * nf
+    part = everyone // nc
+    kq = ka // nc
+    lanes = max(ke, 128)
     cw = min(256, width)
     chunks = width // cw
+    slots = min(8, chunks)
     group = 4
     vmem = pl.BlockSpec(memory_space=pltpu.VMEM)
     hbm = pl.BlockSpec(memory_space=pl.ANY)
     dma = pltpu.SemaphoreType.DMA
-    pooled, cross = pl.pallas_call(
-        functools.partial(conv_kernel, nc, nf, positions, group),
-        out_shape=(
-            jax.ShapeDtypeStruct((images // group, group, width), jnp.float32),
-            jax.ShapeDtypeStruct((images, ka, width), jnp.float32),
-        ),
-        in_specs=[hbm, hbm, hbm, vmem],
-        out_specs=(vmem, vmem),
+    bf16, f32 = jnp.bfloat16, jnp.float32
+    out = pl.pallas_call(
+        functools.partial(trak_kernel, nc, nf, positions, group),
+        out_shape=jax.ShapeDtypeStruct((images, kq, lanes), f32),
+        in_specs=[hbm, hbm, hbm, vmem, hbm, vmem, hbm],
+        out_specs=vmem,
         scratch_shapes=[
-            pltpu.VMEM((nf, chunks, depth, cw), jnp.bfloat16),
-            pltpu.VMEM((nc, rows, share), jnp.bfloat16),
-            pltpu.VMEM((images, ka, positions), jnp.bfloat16),
-            pltpu.VMEM((2, rows, cw), jnp.bfloat16),
+            pltpu.VMEM((nf, chunks, depth, cw), bf16),
+            pltpu.VMEM((nc, rows, share), bf16),
+            pltpu.VMEM((images, ka, positions), bf16),
+            pltpu.VMEM((2, rows, cw), bf16),
+            pltpu.VMEM((chunks, images, ka, cw), bf16),
+            pltpu.VMEM((images, cw), f32),
+            pltpu.VMEM((chunks, nf, images, cw), bf16),
+            pltpu.VMEM((slots, cw, classes), bf16),
+            pltpu.VMEM((nc, part, classes), f32),
+            pltpu.VMEM((nc, part, classes), f32),
+            pltpu.VMEM((nf, part, 128), f32),
+            pltpu.VMEM((nc, part, classes), bf16 if part % 16 == 0 else f32),
+            pltpu.VMEM((chunks, nf, images, cw), bf16),
+            pltpu.VMEM((chunks, nf, images, cw), bf16),
+            pltpu.VMEM((lanes, width), bf16),
+            pltpu.VMEM((images * ka, lanes), f32),
+            pltpu.VMEM((nc, images, kq, lanes), f32),
+            pltpu.VMEM((nc, images, kq, lanes), f32),
             dma((chunks,)),
             dma((nf, chunks)),
             dma((nf, chunks)),
@@ -249,47 +445,34 @@
             dma((nc,)),
             dma,
             dma((2,)),
+            dma((nf, chunks)),
+            dma((nf, chunks)),
+            dma((slots,)),
+            dma((nc,)),
+            dma((nc,)),
+            dma((nf,)),
+            dma((nf,)),
+            dma((nc,)),
+            dma((nc,)),
+            dma((nf, chunks)),
+            dma((nf, chunks)),
+            dma,
+            dma((nc,)),
+            dma((nc,)),
         ],
         compiler_params=pltpu.CompilerParams(
-            collective_id=0, has_side_effects=True, vmem_limit_bytes=56 * 2**20
+            collective_id=0, has_side_effects=True, vmem_limit_bytes=62 * 2**20
         ),
         cost_estimate=pl.CostEstimate(
-            flops=2 * rows * width * depth * nf,
-            bytes_accessed=2 * rows * width + 2 * depth * nf * width,
-            transcendentals=0,
+            flops=2 * rows * width * depth * nf + 4 * everyone * width * classes,
+            bytes_accessed=2 * rows * width + 2 * depth * width + 4 * width * classes,
+            transcendentals=part * classes,
         ),
-    )(stream.reshape(rows, width), mid.reshape(rows, share), weight, proj_t)
-    return pooled.reshape(images, width).astype(jnp.bfloat16), cross
-
-
-def per_device(nc, nf, stream, mid, conv_weight, head_weight, labels, proj_act, proj_err):
-    images, positions, width = stream.shape
-    pooled, cross = conv(stream, mid, conv_weight, proj_act.T, nc, nf)
-    pooled_all = lax.all_gather(pooled, "fsdp", axis=0, tiled=True)
-    partial_value = jnp.dot(pooled_all, head_weight, preferred_element_type=jnp.float32)
-    block = head_weight.shape[1]
-    block_start = lax.axis_index("fsdp") * block
-    logits = lax.psum(partial_value, "chan")
-    expo = jnp.exp(logits)
-    total = lax.psum(jnp.sum(expo, axis=1), "fsdp")
-    classes = block_start + jnp.arange(block, dtype=jnp.int32)
-    onehot = (labels[:, None] == classes[None, :]).astype(jnp.float32)
-    dlogits = (expo / total[:, None] - onehot).astype(jnp.bfloat16)
-    dpooled = lax.psum_scatter(
-        lax.dot_general(
-            dlogits, head_weight, (((1,), (1,)), ((), ())), preferred_element_type=jnp.float32
-        ),
-        "fsdp",
-        scatter_dimension=0,
-        tiled=True,
+    )(
+        stream.reshape(rows, width), mid.reshape(rows, share), conv_weight, proj_act.T,
+        head_weight, labels.reshape(nc, part, 1), proj_err.T,
     )
-    error = (dpooled / positions).astype(jnp.bfloat16).astype(jnp.float32)
-    scaled = (cross * error[:, None, :]).astype(jnp.bfloat16)
-    ka = cross.shape[1]
-    grads = jnp.dot(
-        scaled.reshape(images * ka, width), proj_err, preferred_element_type=jnp.float32
-    ).reshape(images, ka * proj_err.shape[1])
-    return lax.psum_scatter(grads, "chan", scatter_dimension=1, tiled=True)
+    return out[:, :, :ke].reshape(images, kq * ke)
 
 
 def solution(mesh):

time: 441 us -> 343 us (0.78)
  waiting for transfers between devices: 72.8 us -> 0 us
  Pallas kernels: 286 us -> 340 us
  matrix products: 32.5 us -> 0 us
  blocking collectives: 27.5 us -> 0 us
  between operations: 13.2 us -> 0.01 us
  other arithmetic: 7.92 us -> 0 us
    pallas_call x1, Pallas kernels: 286 us -> 340 us  [per_device(): pl.pallas_call(functools.partial(trak_kernel, nc, nf, positions, group),...]
    psum x1 -> x0, waiting for transfers between devices: 39.2 us -> none  [per_device(): logits = lax.psum(partial_value, 'chan')]
    reduce_scatter x2 -> x0, waiting for transfers between devices: 33.6 us -> none  [the longest x1 24.5 us: per_device(): lax.psum_scatter(lax.dot_general(dlogits, head_weight, (((1,), (1,)), (()...]
    dot_general x3 -> x0, matrix products: 32.5 us -> none  [the longest x1 16.7 us: per_device(): lax.dot_general(dlogits, head_weight, (((1,), (1,)), ((), ())), preferred...]
    all_gather x1 -> x0, blocking collectives: 15.8 us -> none  [per_device(): pooled_all = lax.all_gather(pooled, 'fsdp', axis=0, tiled=True)]
    psum x1 -> x0, blocking collectives: 11.7 us -> none  [per_device(): total = lax.psum(jnp.sum(expo, axis=1), 'fsdp')]
    convert_element_type x3 -> x0, other arithmetic: 6.43 us -> none  [the longest x1 4.46 us: per_device(): scaled = (cross * error[:, None, :]).astype(jnp.bfloat16)]
  transfers between devices with their start and end apart: 3 -> 0, of which waited for: 3 -> 0; matrix products, arithmetic and copies ran while one was open for 0% -> 0% of each run, Pallas kernels for 0% -> 0%
where the time goes in v2:
time: 343 us
  Pallas kernels  340 us (99%)
    pallas_call x1, Pallas kernels, per_device(): pl.pallas_call(functools.partial(trak_kernel, nc, nf, positions, group),...  340 us

profile of v2, /device:TPU:0, one launch (start us, length us, event | category | flops | bytes accessed | tf_op | source)
XLA Modules:
  0.0 342.6 jit_solution(15631148867078335237)
XLA Ops:
  0.0 1.4 reshape.16.labels_ref
  1.4 339.5 %shard_map.73 = f32[16,16,128]{2,1,0:T(8,128)} custom-call(bf16[2304,4096]{1,0:T(8,128)(2,1)} %bitcast.6, bf16[2304,1024]{1,0:T(8,128)(2,1)} %bitcast.7, bf16[512,4096]{1,0:T(8,128)(2,1)} %weight_ref.1, bf16[32,2048]{1,0:T(8,128)(2,1)} %bitcast.9, bf16[4096,4096]{1,0:T(8,128)(2,1)} %head_ref.1, s32[2,32,1]{2,1,0:T(8,128)} %reshape.16.labels_ref, ...), custom_call_target="tpu_custom_call" | custom-call | flops 42949672960 | bytes 90177536 | tf_op jit(solution)/shard_map/pallas_call | solution.py:416
  341.0 1.6 reshape.15

commit v3 on v2

--- a/solution.py
+++ b/solution.py
@@ -12,7 +12,7 @@
 
 
 def trak_kernel(
-    nc, nf, positions, group,
+    nc, nf, positions, group, handed,
     stream_ref, mid_ref, weight_ref, proj_ref, head_ref, labels_ref, perr_ref,
     out_ref,
     weights, mids, acts, held, cross, mean, pools, heads, logits, logits_in,
@@ -20,6 +20,7 @@
     own_sem, right_sem, left_sem, in_sem, mid_send, mid_recv, mid_own, held_sem,
     pool_send, pool_recv, head_sem, logit_send, logit_recv, total_send, total_recv,
     dlog_send, dlog_recv, dpool_send, dpool_recv, perr_sem, share_send, share_recv,
+    *handed_refs,
 ):
     c = lax.axis_index("chan")
     f = lax.axis_index("fsdp")
@@ -27,6 +28,49 @@
     share = mids.shape[2]
     rows = mids.shape[1]
     images = rows // positions
+    full = chunks - handed
+    inner = (f > 0) & (f < nf - 1)
+    if handed:
+        (
+            mids_end, streams_end, acts_end, cross_end, piece_send, piece_recv, strip_send, strip_recv,
+            pass_send, pass_recv, pool_end_send, cross_end_send, cross_end_recv,
+        ) = handed_refs
+        inward = jnp.where(f == 0, 1, nf - 2)
+        end = jnp.where(f == 1, 0, nf - 1)
+
+    def served(to, j):
+        return ((to > 0) & (to < nf - 1)) | (j < full)
+
+    def piece_rows(j):
+        return pl.ds(pl.multiple_of(j * positions, 16), positions)
+
+    def piece_copy(j):
+        return pltpu.make_async_remote_copy(
+            src_ref=mid_ref.at[piece_rows(j)], dst_ref=mids_end.at[c, piece_rows(j)],
+            send_sem=piece_send.at[j], recv_sem=piece_recv.at[j],
+            device_id={"fsdp": inward}, device_id_type=MESH,
+        )
+
+    def strip_copy(j):
+        return pltpu.make_async_remote_copy(
+            src_ref=stream_ref.at[piece_rows(j), full * cw :], dst_ref=streams_end.at[piece_rows(j)],
+            send_sem=strip_send.at[j], recv_sem=strip_recv.at[j],
+            device_id={"fsdp": inward}, device_id_type=MESH,
+        )
+
+    def pass_copy(j, d):
+        return pltpu.make_async_remote_copy(
+            src_ref=mids_end.at[c, piece_rows(j)], dst_ref=mids_end.at[c, piece_rows(j)],
+            send_sem=pass_send.at[d, j], recv_sem=pass_recv.at[d, j],
+            device_id={"chan": lax.rem(c + d, nc)}, device_id_type=MESH,
+        )
+
+    def cross_copy(k):
+        return pltpu.make_async_remote_copy(
+            src_ref=cross_end.at[k - full], dst_ref=cross.at[k],
+            send_sem=cross_end_send.at[k - full], recv_sem=cross_end_recv.at[k - full],
+            device_id={"fsdp": end}, device_id_type=MESH,
+        )
 
     def own_copy(j):
         return pltpu.make_async_copy(
@@ -90,7 +134,15 @@
         )
 
     def pool_copy(k, d):
-        return to_fsdp(pools.at[k, f], pools.at[k, f], pool_send.at[d, k], pool_recv.at[d, k], d)
+        return to_fsdp(pools.at[k, f], pools.at[k, f], pool_send.at[d, k], pool_recv.at[f, k], d)
+
+    def pool_end_copy(k, d):
+        return to_fsdp(
+            pools.at[k, end], pools.at[k, end], pool_end_send.at[d, k - full], pool_recv.at[end, k], d
+        )
+
+    def pool_arrival(k, b):
+        return to_fsdp(pools.at[k, b], pools.at[k, b], pool_send.at[1, k], pool_recv.at[b, k], 1)
 
     def logit_copy(d):
         return to_chan(logits.at[lax.rem(c + d, nc)], logits_in.at[c], logit_send, logit_recv, d)
@@ -132,13 +184,19 @@
     def send_own(j):
         own_copy(j).wait()
 
-        @pl.when(f < nf - 1)
+        @pl.when((f < nf - 1) & served(f + 1, j))
         def _():
             hop(f, j, True).start()
 
-        @pl.when(f > 0)
+        @pl.when((f > 0) & served(f - 1, j))
         def _():
             hop(f, j, False).start()
+
+        if handed:
+            @pl.when(jnp.logical_not(inner))
+            def _():
+                piece_copy(j).start()
+                strip_copy(j).start()
 
     for j in range(min(AHEAD, chunks)):
         send_own(j)
@@ -149,37 +207,59 @@
             send_own(r + AHEAD)
 
         for d in range(1, nf):
-            @pl.when(f - d >= 0)
+            @pl.when((f - d >= 0) & served(f, r))
             def _():
                 hop(f - d, r, True).wait_recv()
 
-                @pl.when(f < nf - 1)
+                @pl.when((f < nf - 1) & served(f + 1, r))
                 def _():
                     hop(f - d, r, True).start()
 
-            @pl.when(f + d < nf)
+            @pl.when((f + d < nf) & served(f, r))
             def _():
                 hop(f + d, r, False).wait_recv()
 
-                @pl.when(f > 0)
+                @pl.when((f > 0) & served(f - 1, r))
                 def _():
                     hop(f + d, r, False).start()
 
+        if handed:
+            @pl.when(inner & (r >= chunks // 2))
+            def _():
+                for q in range(2):
+                    j = 2 * (r - chunks // 2) + q
+                    piece_copy(j).wait_recv()
+                    for d in range(1, nc):
+                        pass_copy(j, d).start()
+
     step = min(depth, share)
     pieces = nf * depth // step
 
     def compute(k):
         stream_copy(k).wait()
 
-        @pl.when(k + 1 < chunks)
+        @pl.when((k + 1 < chunks) & served(f, k + 1))
         def _():
             stream_copy(k + 1).start()
 
         slot = lax.rem(k, 2)
-
+        convolve(k, mids, acts, lambda span: held[slot, span, :], cross.at[k])
+        pools[k, f] = mean[...].astype(jnp.bfloat16)
+        for d in range(1, nf):
+            pool_copy(k, d).start()
+
+    def compute_end(k):
+        at = (k - full) * cw
+        convolve(k, mids_end, acts_end, lambda span: streams_end[span, at : at + cw], cross_end.at[k - full])
+        pools[k, end] = mean[...].astype(jnp.bfloat16)
+        for d in range(1, nf):
+            pool_end_copy(k, d).start()
+        cross_copy(k).start()
+
+    def convolve(k, mids, acts, load, sums):
         def some(g, x):
             span = pl.ds(pl.multiple_of(g * group * positions, 16), group * positions)
-            y = held[slot, span, :].astype(jnp.float32)
+            y = load(span).astype(jnp.float32)
             for s in range(pieces):
                 at = s * step
                 y += jnp.dot(
@@ -192,20 +272,24 @@
                 total = jnp.sum(jnp.maximum(one, 0.0), axis=0, keepdims=True)
                 mean[pl.ds(g * group + i, 1), :] = total / positions
                 mask = jnp.where(one > 0.0, 1.0, 0.0).astype(jnp.bfloat16)
-                cross[k, g * group + i] = jnp.dot(
+                sums[g * group + i] = jnp.dot(
                     acts[g * group + i], mask, preferred_element_type=jnp.float32
-                ).astype(cross.dtype)
+                ).astype(sums.dtype)
             return x
 
         lax.fori_loop(0, images // group, some, 0)
-        pools[k, f] = mean[...].astype(jnp.bfloat16)
-        for d in range(1, nf):
-            pool_copy(k, d).start()
-
-    def add_logits(k):
+
+    def add_logits(k, late=False):
         head_copy(k).wait()
-        for d in range(1, nf):
-            pool_copy(k, d).wait_recv()
+        for b in range(nf):
+            here = f == b
+            if late:
+                here = inner & (here | (end == b))
+
+            @pl.when(jnp.logical_not(here))
+            def _():
+                pool_arrival(k, b).wait_recv()
+
         slot = lax.rem(k, slots)
         rows_all = pools[k].reshape(nf * images, cw)
 
@@ -219,11 +303,7 @@
         lax.fori_loop(0, classes // tile, some, 0)
         head_copy(k + slots).start()
 
-    def project():
-        own_mid.wait()
-        for d in range(1, nc):
-            mid_copy(d).wait_recv()
-
+    def project(mids, acts):
         def one(i, x):
             span = pl.ds(pl.multiple_of(i * positions, 16), positions)
             out = jnp.zeros((proj_ref.shape[0], positions), jnp.float32)
@@ -237,10 +317,13 @@
 
         lax.fori_loop(0, images, one, 0)
 
-    first = max(chunks // 2 - 1, 0)
-    last = max(chunks - 2, 0)
+    first = max(full // 2 - 1, 0)
+    last = max(full - 2, 0)
     lax.fori_loop(0, first, lambda r, x: (relay(r), x)[1], 0)
-    project()
+    own_mid.wait()
+    for d in range(1, nc):
+        mid_copy(d).wait_recv()
+    project(mids, acts)
 
     def pair(r, x):
         relay(r)
@@ -266,9 +349,27 @@
 
         return x
 
-    lax.fori_loop(last, chunks, single, 0)
+    lax.fori_loop(last, full, single, 0)
+    if handed:
+        @pl.when(inner)
+        def _():
+            for r in range(full, chunks):
+                relay(r)
+                compute(r)
+
+            def arrived(j, x):
+                strip_copy(j).wait_recv()
+                for d in range(1, nc):
+                    pass_copy(j, d).wait_recv()
+                return x
+
+            lax.fori_loop(0, images, arrived, 0)
+            project(mids_end, acts_end)
+            for k in range(full, chunks):
+                compute_end(k)
+
     for k in range(last, chunks):
-        add_logits(k)
+        add_logits(k, k >= full)
 
     for d in range(1, nc):
         logit_copy(d).start()
@@ -323,6 +424,12 @@
         return x
 
     lax.fori_loop(0, chunks, back, 0)
+    if handed:
+        @pl.when(jnp.logical_not(inner))
+        def _():
+            for k in range(full, chunks):
+                cross_copy(k).wait_recv()
+
     perr_copy.wait()
     grads[...] = jnp.zeros_like(grads)
 
@@ -362,27 +469,47 @@
     out_ref[...] = result
 
     def drain(j, x):
-        @pl.when(f < nf - 1)
-        def _():
-            hop(f, j, True).wait_send()
-
-        @pl.when(f > 0)
-        def _():
-            hop(f, j, False).wait_send()
+        @pl.when((f < nf - 1) & served(f + 1, j))
+        def _():
+            for d in range(nf):
+                @pl.when(f - d >= 0)
+                def _():
+                    hop(f - d, j, True).wait_send()
+
+        @pl.when((f > 0) & served(f - 1, j))
+        def _():
+            for d in range(nf):
+                @pl.when(f + d < nf)
+                def _():
+                    hop(f + d, j, False).wait_send()
 
         for d in range(1, nf):
-            pool_copy(j, d).wait_send()
             dpool_copy(j, d).wait_send()
 
-            @pl.when((f - d >= 0) & (f < nf - 1))
-            def _():
-                hop(f - d, j, True).wait_send()
-
-            @pl.when((f + d < nf) & (f > 0))
-            def _():
-                hop(f + d, j, False).wait_send()
+            @pl.when(served(f, j))
+            def _():
+                pool_copy(j, d).wait_send()
+
+        if handed:
+            @pl.when(jnp.logical_not(inner))
+            def _():
+                piece_copy(j).wait_send()
+                strip_copy(j).wait_send()
+
+            @pl.when(inner)
+            def _():
+                for d in range(1, nc):
+                    pass_copy(j, d).wait_send()
 
         return x
+
+    if handed:
+        @pl.when(inner)
+        def _():
+            for k in range(full, chunks):
+                cross_copy(k).wait_send()
+                for d in range(1, nf):
+                    pool_end_copy(k, d).wait_send()
 
     lax.fori_loop(0, chunks, drain, 0)
     for d in range(1, nc):
@@ -407,14 +534,15 @@
     lanes = max(ke, 128)
     cw = min(256, width)
     chunks = width // cw
-    slots = min(8, chunks)
+    slots = min(4, chunks)
+    handed = 2 if nf == 4 and chunks == images and chunks >= 16 else 0
     group = 4
     vmem = pl.BlockSpec(memory_space=pltpu.VMEM)
     hbm = pl.BlockSpec(memory_space=pl.ANY)
     dma = pltpu.SemaphoreType.DMA
     bf16, f32 = jnp.bfloat16, jnp.float32
     out = pl.pallas_call(
-        functools.partial(trak_kernel, nc, nf, positions, group),
+        functools.partial(trak_kernel, nc, nf, positions, group, handed),
         out_shape=jax.ShapeDtypeStruct((images, kq, lanes), f32),
         in_specs=[hbm, hbm, hbm, vmem, hbm, vmem, hbm],
         out_specs=vmem,
@@ -459,7 +587,21 @@
             dma,
             dma((nc,)),
             dma((nc,)),
-        ],
+        ] + ([
+            pltpu.VMEM((nc, rows, share), bf16),
+            pltpu.VMEM((rows, handed * cw), bf16),
+            pltpu.VMEM((images, ka, positions), bf16),
+            pltpu.VMEM((handed, images, ka, cw), bf16),
+            dma((chunks,)),
+            dma((chunks,)),
+            dma((chunks,)),
+            dma((chunks,)),
+            dma((nc, chunks)),
+            dma((nc, chunks)),
+            dma((nf, handed)),
+            dma((handed,)),
+            dma((handed,)),
+        ] if handed else []),
         compiler_params=pltpu.CompilerParams(
             collective_id=0, has_side_effects=True, vmem_limit_bytes=62 * 2**20
         ),

time: 343 us -> 364 us (1.061)
  Pallas kernels: 340 us -> 360 us
    pallas_call x1, Pallas kernels: 340 us -> 360 us  [per_device(): pl.pallas_call(functools.partial(trak_kernel, nc, nf, positions, group, h...]
where the time goes in v3:
time: 364 us
  Pallas kernels  360 us (99%)
    pallas_call x1, Pallas kernels, per_device(): pl.pallas_call(functools.partial(trak_kernel, nc, nf, positions, group, h...  360 us

profile of v3, /device:TPU:0, one launch (start us, length us, event | category | flops | bytes accessed | tf_op | source)
XLA Modules:
  0.0 363.5 jit_solution(5384409308059938389)
XLA Ops:
  0.0 1.4 reshape.16.labels_ref
  1.4 360.5 %shard_map.73 = f32[16,16,128]{2,1,0:T(8,128)} custom-call(bf16[2304,4096]{1,0:T(8,128)(2,1)} %bitcast.6, bf16[2304,1024]{1,0:T(8,128)(2,1)} %bitcast.7, bf16[512,4096]{1,0:T(8,128)(2,1)} %weight_ref.1, bf16[32,2048]{1,0:T(8,128)(2,1)} %bitcast.9, bf16[4096,4096]{1,0:T(8,128)(2,1)} %head_ref.1, s32[2,32,1]{2,1,0:T(8,128)} %reshape.16.labels_ref, ...), custom_call_target="tpu_custom_call" | custom-call | flops 42949672960 | bytes 90177536 | tf_op jit(solution)/shard_map/pallas_call | solution.py:544
  361.9 1.6 reshape.15

commit v4 on v3

--- a/solution.py
+++ b/solution.py
@@ -144,14 +144,18 @@
     def pool_arrival(k, b):
         return to_fsdp(pools.at[k, b], pools.at[k, b], pool_send.at[1, k], pool_recv.at[b, k], 1)
 
-    def logit_copy(d):
-        return to_chan(logits.at[lax.rem(c + d, nc)], logits_in.at[c], logit_send, logit_recv, d)
+    def logit_copy(d, g):
+        span = pl.ds(pl.multiple_of(g * tile, tile), tile)
+        return to_chan(
+            logits.at[lax.rem(c + d, nc), :, span], logits_in.at[c, :, span], logit_send.at[g], logit_recv.at[g], d
+        )
 
     def total_copy(d):
         return to_fsdp(totals.at[f], totals.at[f], total_send.at[d], total_recv.at[d], d)
 
-    def dlog_copy(d):
-        return to_chan(dlogits.at[c], dlogits.at[c], dlog_send, dlog_recv, d)
+    def dlog_copy(d, g):
+        span = pl.ds(pl.multiple_of(g * tile, tile), tile)
+        return to_chan(dlogits.at[c, :, span], dlogits.at[c, :, span], dlog_send.at[g], dlog_recv.at[g], d)
 
     def dpool_copy(k, d):
         return to_fsdp(
@@ -279,7 +283,7 @@
 
         lax.fori_loop(0, images // group, some, 0)
 
-    def add_logits(k, late=False):
+    def add_logits(k, late=False, final=False):
         head_copy(k).wait()
         for b in range(nf):
             here = f == b
@@ -298,6 +302,9 @@
             add = jnp.dot(rows_all, heads[slot, :, span], preferred_element_type=jnp.float32)
             for q in range(nc):
                 logits[q, :, span] += add[q * part : (q + 1) * part]
+            if final:
+                for d in range(1, nc):
+                    logit_copy(d, g).start()
             return x
 
         lax.fori_loop(0, classes // tile, some, 0)
@@ -317,8 +324,8 @@
 
         lax.fori_loop(0, images, one, 0)
 
-    first = max(full // 2 - 1, 0)
-    last = max(full - 2, 0)
+    last = max(full - 2, 0) // 2 * 2
+    first = last // 2
     lax.fori_loop(0, first, lambda r, x: (relay(r), x)[1], 0)
     own_mid.wait()
     for d in range(1, nc):
@@ -368,15 +375,49 @@
             for k in range(full, chunks):
                 compute_end(k)
 
-    for k in range(last, chunks):
-        add_logits(k, k >= full)
-
-    for d in range(1, nc):
-        logit_copy(d).start()
-    for d in range(1, nc):
-        logit_copy(d).wait_recv()
+    for k in range(max(full - 2, 0), chunks):
+        add_logits(k, k >= full, k == chunks - 1)
+
+    def drain(j, x):
+        @pl.when((f < nf - 1) & served(f + 1, j))
+        def _():
+            for d in range(nf):
+                @pl.when(f - d >= 0)
+                def _():
+                    hop(f - d, j, True).wait_send()
+
+        @pl.when((f > 0) & served(f - 1, j))
+        def _():
+            for d in range(nf):
+                @pl.when(f + d < nf)
+                def _():
+                    hop(f + d, j, False).wait_send()
+
+        @pl.when(served(f, j))
+        def _():
+            for d in range(1, nf):
+                pool_copy(j, d).wait_send()
+
+        if handed:
+            @pl.when(jnp.logical_not(inner))
+            def _():
+                piece_copy(j).wait_send()
+                strip_copy(j).wait_send()
+
+            @pl.when(inner)
+            def _():
+                for d in range(1, nc):
+                    pass_copy(j, d).wait_send()
+
+        return x
+
+    lax.fori_loop(0, chunks, drain, 0)
+    for d in range(1, nc):
+        mid_copy(d).wait_send()
 
     def exponents(g, total):
+        for d in range(1, nc):
+            logit_copy(d, g).wait_recv()
         span = pl.ds(pl.multiple_of(g * tile, tile), tile)
         value = logits[c, :, span]
         for d in range(1, nc):
@@ -398,21 +439,34 @@
         ids = f * classes + g * tile + lax.broadcasted_iota(jnp.int32, (part, tile), 1)
         onehot = jnp.where(labels_ref[c] == ids, 1.0, 0.0)
         dlogits[c, :, span] = (logits[c, :, span] / total - onehot).astype(dlogits.dtype)
+        for d in range(1, nc):
+            dlog_copy(d, g).start()
         return x
 
     lax.fori_loop(0, classes // tile, derivatives, 0)
-    for d in range(1, nc):
-        dlog_copy(d).start()
-    for d in range(1, nc):
-        dlog_copy(d).wait_recv()
+    for g in range(classes // tile):
+        for d in range(1, nc):
+            dlog_copy(d, g).wait_recv()
+    perr_copy.wait()
+    grads[...] = jnp.zeros_like(grads)
+    if handed:
+        @pl.when(jnp.logical_not(inner))
+        def _():
+            for k in range(full, chunks):
+                cross_copy(k).wait_recv()
+
 
     def back(k, x):
         head_copy(k + chunks).wait()
+        if x is not None:
+            arrivals(k - lag)
         slot = lax.rem(k + chunks, slots)
         grad = lax.dot_general(
             dlogits[...].reshape(nc * part, classes).astype(jnp.bfloat16), heads[slot],
             (((1,), (1,)), ((), ())), preferred_element_type=jnp.float32,
         )
+        if x is not None:
+            finish(k - lag)
         dpool[k] = grad.reshape(nf, images, cw).astype(jnp.bfloat16)
         for d in range(1, nf):
             dpool_copy(k, d).start()
@@ -423,20 +477,14 @@
 
         return x
 
-    lax.fori_loop(0, chunks, back, 0)
-    if handed:
-        @pl.when(jnp.logical_not(inner))
-        def _():
-            for k in range(full, chunks):
-                cross_copy(k).wait_recv()
-
-    perr_copy.wait()
-    grads[...] = jnp.zeros_like(grads)
-
-    def finish(k, x):
-        error = dpool[k, f].astype(jnp.float32)
+    lag = min(4, chunks)
+
+    def arrivals(k):
         for d in range(1, nf):
             dpool_copy(k, d).wait_recv()
+
+    def finish(k):
+        error = dpool[k, f].astype(jnp.float32)
         for d in range(1, nf):
             error += dpool_in[k, lax.rem(f + nf - d, nf)].astype(jnp.float32)
         error = (error / positions).astype(jnp.bfloat16).astype(jnp.float32)
@@ -451,9 +499,13 @@
             scaled, perr[:, pl.ds(pl.multiple_of(k * cw, cw), cw)],
             (((1,), (1,)), ((), ())), preferred_element_type=jnp.float32,
         )
-        return x
-
-    lax.fori_loop(0, chunks, finish, 0)
+
+    for k in range(lag):
+        back(k, None)
+    lax.fori_loop(lag, chunks, back, 0)
+    for k in range(chunks - lag, chunks):
+        arrivals(k)
+        finish(k)
     ka = proj_ref.shape[0]
     kq = ka // nc
     for q in range(nc):
@@ -468,41 +520,6 @@
         result += shares_in[lax.rem(c + nc - d, nc)]
     out_ref[...] = result
 
-    def drain(j, x):
-        @pl.when((f < nf - 1) & served(f + 1, j))
-        def _():
-            for d in range(nf):
-                @pl.when(f - d >= 0)
-                def _():
-                    hop(f - d, j, True).wait_send()
-
-        @pl.when((f > 0) & served(f - 1, j))
-        def _():
-            for d in range(nf):
-                @pl.when(f + d < nf)
-                def _():
-                    hop(f + d, j, False).wait_send()
-
-        for d in range(1, nf):
-            dpool_copy(j, d).wait_send()
-
-            @pl.when(served(f, j))
-            def _():
-                pool_copy(j, d).wait_send()
-
-        if handed:
-            @pl.when(jnp.logical_not(inner))
-            def _():
-                piece_copy(j).wait_send()
-                strip_copy(j).wait_send()
-
-            @pl.when(inner)
-            def _():
-                for d in range(1, nc):
-                    pass_copy(j, d).wait_send()
-
-        return x
-
     if handed:
         @pl.when(inner)
         def _():
@@ -511,11 +528,16 @@
                 for d in range(1, nf):
                     pool_end_copy(k, d).wait_send()
 
-    lax.fori_loop(0, chunks, drain, 0)
-    for d in range(1, nc):
-        mid_copy(d).wait_send()
-        logit_copy(d).wait_send()
-        dlog_copy(d).wait_send()
+    def drain_late(j, x):
+        for d in range(1, nf):
+            dpool_copy(j, d).wait_send()
+        return x
+
+    lax.fori_loop(0, chunks, drain_late, 0)
+    for d in range(1, nc):
+        for g in range(classes // tile):
+            logit_copy(d, g).wait_send()
+            dlog_copy(d, g).wait_send()
         share_copy(d).wait_send()
     for d in range(1, nf):
         total_copy(d).wait_send()
@@ -534,8 +556,8 @@
     lanes = max(ke, 128)
     cw = min(256, width)
     chunks = width // cw
-    slots = min(4, chunks)
-    handed = 2 if nf == 4 and chunks == images and chunks >= 16 else 0
+    slots = min(8, chunks)
+    handed = 0
     group = 4
     vmem = pl.BlockSpec(memory_space=pltpu.VMEM)
     hbm = pl.BlockSpec(memory_space=pl.ANY)
@@ -576,12 +598,12 @@
             dma((nf, chunks)),
             dma((nf, chunks)),
             dma((slots,)),
-            dma((nc,)),
-            dma((nc,)),
+            dma((classes // min(1024, classes), nc)),
+            dma((classes // min(1024, classes), nc)),
             dma((nf,)),
             dma((nf,)),
-            dma((nc,)),
-            dma((nc,)),
+            dma((classes // min(1024, classes), nc)),
+            dma((classes // min(1024, classes), nc)),
             dma((nf, chunks)),
             dma((nf, chunks)),
             dma,

time: 364 us -> 347 us (0.953)
  Pallas kernels: 360 us -> 344 us
    pallas_call x1, Pallas kernels: 360 us -> 344 us  [per_device(): pl.pallas_call(functools.partial(trak_kernel, nc, nf, positions, group, h...]
where the time goes in v4:
time: 347 us
  Pallas kernels  344 us (99%)
    pallas_call x1, Pallas kernels, per_device(): pl.pallas_call(functools.partial(trak_kernel, nc, nf, positions, group, h...  344 us

profile of v4, /device:TPU:0, one launch (start us, length us, event | category | flops | bytes accessed | tf_op | source)
XLA Modules:
  0.0 347.2 jit_solution(4998129079855234302)
XLA Ops:
  0.0 1.4 reshape.16.labels_ref
  1.4 344.2 %shard_map.73 = f32[16,16,128]{2,1,0:T(8,128)} custom-call(bf16[2304,4096]{1,0:T(8,128)(2,1)} %bitcast.6, bf16[2304,1024]{1,0:T(8,128)(2,1)} %bitcast.7, bf16[512,4096]{1,0:T(8,128)(2,1)} %weight_ref.1, bf16[32,2048]{1,0:T(8,128)(2,1)} %bitcast.9, bf16[4096,4096]{1,0:T(8,128)(2,1)} %head_ref.1, s32[2,32,1]{2,1,0:T(8,128)} %reshape.16.labels_ref, ...), custom_call_target="tpu_custom_call" | custom-call | flops 42949672960 | bytes 90177536 | tf_op jit(solution)/shard_map/pallas_call | solution.py:566
  345.6 1.6 reshape.15

commit v5 on v2

--- a/solution.py
+++ b/solution.py
@@ -237,6 +237,7 @@
 
         lax.fori_loop(0, images, one, 0)
 
+    end = (f == 0) | (f == nf - 1)
     first = max(chunks // 2 - 1, 0)
     last = max(chunks - 2, 0)
     lax.fori_loop(0, first, lambda r, x: (relay(r), x)[1], 0)
@@ -247,10 +248,15 @@
         compute(2 * (r - first))
         compute(2 * (r - first) + 1)
 
-        @pl.when(r > first)
+        @pl.when(end & (r > first))
         def _():
             add_logits(2 * (r - first) - 2)
             add_logits(2 * (r - first) - 1)
+
+        @pl.when(jnp.logical_not(end) & (r > first + 1))
+        def _():
+            add_logits(2 * (r - first) - 4)
+            add_logits(2 * (r - first) - 3)
 
         return x
 
@@ -260,13 +266,18 @@
         relay(r)
         compute(r)
 
-        @pl.when(r >= 2)
+        @pl.when(end & (r >= 2))
         def _():
             add_logits(r - 2)
 
         return x
 
     lax.fori_loop(last, chunks, single, 0)
+
+    @pl.when(jnp.logical_not(end))
+    def _():
+        lax.fori_loop(max(last - 4, 0), last, lambda k, x: (add_logits(k), x)[1], 0)
+
     for k in range(last, chunks):
         add_logits(k)
 

time: 343 us -> 344 us (level)
  no operation moved by 1% of the time
where the time goes in v5:
time: 344 us
  Pallas kernels  341 us (99%)
    pallas_call x1, Pallas kernels, per_device(): pl.pallas_call(functools.partial(trak_kernel, nc, nf, positions, group),...  341 us

profile of v5, /device:TPU:0, one launch (start us, length us, event | category | flops | bytes accessed | tf_op | source)
XLA Modules:
  0.0 343.7 jit_solution(721715797051354678)
XLA Ops:
  0.0 1.4 reshape.16.labels_ref
  1.4 340.7 %shard_map.73 = f32[16,16,128]{2,1,0:T(8,128)} custom-call(bf16[2304,4096]{1,0:T(8,128)(2,1)} %bitcast.6, bf16[2304,1024]{1,0:T(8,128)(2,1)} %bitcast.7, bf16[512,4096]{1,0:T(8,128)(2,1)} %weight_ref.1, bf16[32,2048]{1,0:T(8,128)(2,1)} %bitcast.9, bf16[4096,4096]{1,0:T(8,128)(2,1)} %head_ref.1, s32[2,32,1]{2,1,0:T(8,128)} %reshape.16.labels_ref, ...), custom_call_target="tpu_custom_call" | custom-call | flops 42949672960 | bytes 90177536 | tf_op jit(solution)/shard_map/pallas_call | solution.py:427
  342.1 1.6 reshape.15
